TPU v7x, 32 devices: a whole 2x2x4 slice. The times are simulated.
32 devices in a mesh: dp: 16 (over z, x, core), expert: 2 (over y).
Axes of the slice: x: 2, y: 2, z: 4, core: 2. Of those that a mesh axis runs over, the one named last changes fastest.
Arguments:
- tokens: bfloat16 [8192, 2560], P(('dp', 'expert')), may hold values from -6 to 6
- routes: int32 [8192, 1], P(('dp', 'expert')), may hold values from 0 to 1; in each aligned block of 256 rows (0 to 255, 256 to 511, ...) at most 160 rows name the same one
- gate_levels: int32 [8192, 1], P(('dp', 'expert')), may hold values from 1 to 64
- w_gate: bfloat16 [2, 2560, 768], P('expert', 'dp'), may hold values from -0.125 to 0.125
- w_up: bfloat16 [2, 2560, 768], P('expert', 'dp'), may hold values from -0.125 to 0.125
- w_down: bfloat16 [2, 2560, 768], P('expert', 'dp'), may hold values from -0.21875 to 0.21875
- grad_out: bfloat16 [8192, 2560], P(('dp', 'expert')), may hold values from -6 to 6
Outputs:
- moe_out: bfloat16 [8192, 2560], P(('dp', 'expert'))
- grad_tokens: bfloat16 [8192, 2560], P(('dp', 'expert'))
- grad_gate: float32 [2, 2560, 768], P('expert', 'dp')
- grad_up: float32 [2, 2560, 768], P('expert', 'dp')
- grad_down: float32 [2, 2560, 768], P('expert', 'dp')
Inputs may be any that keep to these rules, and one draw needn't show every extreme that they name: `routes`: among the rows of one device, no expert is named by more than 160 tokens, a bound that some block reaches.
All inputs are finite; a program needn't handle non-finite values.
Results may differ from a plain program's by a relative error of at most 0.019.
Values may be sent and summed in bfloat16 or wider, within the bound.
A program may use at most 128 MiB of HBM per device.

v0:
```python
import jax
import jax.numpy as jnp
from jax import lax
from jax.sharding import PartitionSpec as P

TOP = 1


def contract_last(matrix_a, matrix_b):
    return lax.dot_general(
        matrix_a, matrix_b, (((1,), (1,)), ((), ())), preferred_element_type=jnp.float32
    )


def contract_first(matrix_a, matrix_b):
    return lax.dot_general(
        matrix_a, matrix_b, (((0,), (0,)), ((), ())), preferred_element_type=jnp.float32
    )


def shards(tokens, routes, gate_levels, w_gate, w_up, w_down, grad_out):
    experts = lax.axis_size("expert")
    tok_rows = tokens.shape[0]
    model_width = tokens.shape[1]
    capacity = min(tok_rows, tok_rows * TOP * 5 // (4 * experts))
    slot_count = experts * capacity
    expert_of = routes[:, 0]
    onehot = (expert_of[:, None] == jnp.arange(experts, dtype=jnp.int32)[None, :]).astype(jnp.int32)
    earlier = jnp.cumsum(onehot, axis=0) - onehot
    slot_rank = jnp.sum(earlier * onehot, axis=1)
    slot_index = expert_of * capacity + slot_rank
    source_row = (
        jnp.zeros((slot_count,), jnp.int32)
        .at[slot_index]
        .set(jnp.arange(tok_rows, dtype=jnp.int32))
    )
    filled = (
        jnp.zeros((slot_count, 1), jnp.bfloat16)
        .at[slot_index, 0]
        .set(jnp.ones((tok_rows,), jnp.bfloat16))
    )
    gate_weight = gate_levels.astype(jnp.float32) / 64.0

    def pack_rows(values):
        return (jnp.take(values, source_row, axis=0) * filled).reshape(
            experts, capacity, model_width
        )

    trio_full = (
        lax.all_gather(w_gate, "dp", axis=1, tiled=True),
        lax.all_gather(w_up, "dp", axis=1, tiled=True),
        lax.all_gather(w_down, "dp", axis=1, tiled=True),
    )
    gate_full = trio_full[0][0]
    up_full = trio_full[1][0]
    down_full = trio_full[2][0]
    received = lax.all_to_all(
        pack_rows(tokens), "expert", split_axis=0, concat_axis=0, tiled=True
    ).reshape(slot_count, model_width)
    act_gate = jnp.dot(received, gate_full, preferred_element_type=jnp.float32)
    act_up = jnp.dot(received, up_full, preferred_element_type=jnp.float32)
    sigmoid_gate = jax.nn.sigmoid(act_gate)
    silu_gate = act_gate * sigmoid_gate
    hidden = (silu_gate * act_up).astype(jnp.bfloat16)
    expert_out = (
        contract_last(hidden, down_full)
        .astype(jnp.bfloat16)
        .reshape(experts, capacity, model_width)
    )
    returned = lax.all_to_all(
        expert_out, "expert", split_axis=0, concat_axis=0, tiled=True
    ).reshape(slot_count, model_width)
    moe_out = (gate_weight * jnp.take(returned, slot_index, axis=0).astype(jnp.float32)).astype(
        jnp.bfloat16
    )
    out_grad = (gate_weight * grad_out.astype(jnp.float32)).astype(jnp.bfloat16)
    grad_rows = lax.all_to_all(
        pack_rows(out_grad), "expert", split_axis=0, concat_axis=0, tiled=True
    ).reshape(slot_count, model_width)
    hidden_grad = jnp.dot(grad_rows, down_full, preferred_element_type=jnp.float32)
    gate_delta = (
        hidden_grad * act_up * sigmoid_gate * (1.0 + act_gate * (1.0 - sigmoid_gate))
    ).astype(jnp.bfloat16)
    up_delta = (hidden_grad * silu_gate).astype(jnp.bfloat16)
    token_grad = (contract_last(gate_delta, gate_full) + contract_last(up_delta, up_full)).astype(
        jnp.bfloat16
    )
    arrived = lax.all_to_all(
        token_grad.reshape(experts, capacity, model_width),
        "expert",
        split_axis=0,
        concat_axis=0,
        tiled=True,
    )
    grad_tokens = jnp.take(arrived.reshape(slot_count, model_width), slot_index, axis=0)
    part_gate = contract_first(received, gate_delta).astype(jnp.bfloat16)
    part_up = contract_first(received, up_delta).astype(jnp.bfloat16)
    part_down = contract_first(grad_rows, hidden).astype(jnp.bfloat16)
    shares = (
        lax.psum_scatter(part_gate, "dp", scatter_dimension=0, tiled=True).astype(jnp.float32),
        lax.psum_scatter(part_up, "dp", scatter_dimension=0, tiled=True).astype(jnp.float32),
        lax.psum_scatter(part_down, "dp", scatter_dimension=0, tiled=True).astype(jnp.float32),
    )
    grad_gate = shares[0]
    grad_up = shares[1]
    grad_down = shares[2]
    return (moe_out, grad_tokens, grad_gate[None], grad_up[None], grad_down[None])


def solution(mesh):
    in_specs = (
        P(("dp", "expert"), None),
        P(("dp", "expert"), None),
        P(("dp", "expert"), None),
        P("expert", "dp", None),
        P("expert", "dp", None),
        P("expert", "dp", None),
        P(("dp", "expert"), None),
    )
    out_specs = (
        P(("dp", "expert"), None),
        P(("dp", "expert"), None),
        P("expert", "dp", None),
        P("expert", "dp", None),
        P("expert", "dp", None),
    )
    return jax.shard_map(shards, mesh=mesh, in_specs=in_specs, out_specs=out_specs, check_vma=False)
```

profile of v0, /device:TPU:0, one launch (start us, length us, event | category | flops | bytes accessed | tf_op | source)
XLA Modules:
  0.0 396.8 jit_solution(18290300575393256431)
XLA Ops:
  7.2 0.0 copy-start
  7.2 0.0 all-gather.4.cloned.1.call-start
  7.2 0.7 all-gather.4.cloned.1.call-update
  7.9 0.0 all-gather.6.cloned.1.call-start
  8.0 0.7 all-gather.6.cloned.1.call-update
  8.7 0.0 all-gather.8.cloned.1.call-start
  8.7 0.7 all-gather.8.cloned.1.call-update
  9.4 0.7 compare_convert_fusion
  10.1 0.6 reduce-window.6
  10.7 0.2 slice_reduce_fusion
  10.9 0.2 reduce-window.9
  11.1 0.1 add_bitcast_fusion
  11.2 0.7 fusion.14
  11.9 0.7 compare_select_fusion
  12.6 1.4 scatter_custom_fusion
  14.0 0.7 convert_multiply_fusion
  14.7 1.6 multiply_convert_fusion
  16.3 3.2 gather_fusion.2
  19.5 0.0 copy-done
  19.5 3.2 gather_fusion
  22.7 2.2 scatter_custom_fusion.1
  24.8 0.0 copy-done.1
  24.9 3.0 select_multiply_fusion
  27.9 24.7 %all_to_all.20 = bf16[2,160,2560]{2,1,0:T(8,128)(2,1)} all-to-all(bf16[2,160,2560]{2,1,0:T(8,128)(2,1)S(1)} %bitcast.71), channel_id=1, replica_groups=mesh['dp'=16,'expert'=2] {'expert'}, dimensions={0} | all-to-all | bytes 3276800 | tf_op jit(solution)/shard_map/all_to_all | solution.py:57
  52.6 3.7 all-to-all-start.2
  56.3 0.0 reduce-scatter.4.cloned.1.call-start
  56.4 5.4 %all-gather.4.cloned.1.call-done = bf16[1,2560,768]{2,1,0:T(8,128)(2,1)} async-done(((bf16[1,160,768]{2,1,0:T(8,128)(2,1)}), bf16[1,2560,768]{2,1,0:T(8,128)(2,1)}) %all-gather.4.cloned.1.call-update) | async-done | bytes 3932176 | tf_op jit(solution)/shard_map/all_gather | solution.py:50
  61.8 5.0 %fusion.9 = f32[320,768]{1,0:T(8,128)} fusion(bf16[320,2560]{1,0:T(8,128)(2,1)} %bitcast.74, bf16[1,2560,768]{2,1,0:T(8,128)(2,1)} %all-gather.4.cloned.1.call-done), kind=kOutput, calls=%fused_computation.20 | convolution fusion | flops 1258291200 | bytes 6553600 | tf_op jit(solution)/shard_map/dot_general | solution.py:60
  66.8 45.2 %all-gather.6.cloned.1.call-done = bf16[1,2560,768]{2,1,0:T(8,128)(2,1)} async-done(((bf16[1,160,768]{2,1,0:T(8,128)(2,1)}), bf16[1,2560,768]{2,1,0:T(8,128)(2,1)}) %all-gather.6.cloned.1.call-update) | async-done | bytes 3932176 | tf_op jit(solution)/shard_map/all_gather | solution.py:51
  112.0 5.0 %fusion.5 = f32[320,768]{1,0:T(8,128)} fusion(bf16[320,2560]{1,0:T(8,128)(2,1)} %bitcast.75, bf16[1,2560,768]{2,1,0:T(8,128)(2,1)} %all-gather.6.cloned.1.call-done), kind=kOutput, calls=%fused_computation.16 | convolution fusion | flops 1258291200 | bytes 6553600 | tf_op jit(solution)/shard_map/dot_general | solution.py:61
  117.0 0.0 all-to-all-done.2
  117.0 45.2 %all-gather.8.cloned.1.call-done = bf16[1,2560,768]{2,1,0:T(8,128)(2,1)} async-done(((bf16[1,160,768]{2,1,0:T(8,128)(2,1)}), bf16[1,2560,768]{2,1,0:T(8,128)(2,1)}) %all-gather.8.cloned.1.call-update) | async-done | bytes 3932176 | tf_op jit(solution)/shard_map/all_gather | solution.py:52
  162.2 5.4 %multiply_convert_fusion.2 = (bf16[320,768]{1,0:T(8,128)(2,1)}, bf16[320,768]{1,0:T(8,128)(2,1)S(1)}, bf16[320,768]{1,0:T(8,128)(2,1)}) fusion(f32[320,768]{1,0:T(8,128)} %fusion.9, f32[320,768]{1,0:T(8,128)} %fusion.5, bf16[320,2560]{1,0:T(8,128)(2,1)S(1)} %bitcast.72, bf16[1,2560,768]{2,1,0:T(8,128)(2,1)} %all-gather.8.cloned.1.call-done), kind=kOutput, calls=%fused_computation.27 | convolution fusion | flops 1261977600 | bytes 9011200 | tf_op jit(solution)/shard_map/dot_general | solution.py:80
  167.6 0.0 copy-done.3
  167.6 4.2 %convolution_convert_fusion.2 = bf16[2560,768]{1,0:T(8,128)(2,1)} fusion(bf16[320,2560]{1,0:T(8,128)(2,1)S(1)} %bitcast.77, bf16[320,768]{1,0:T(8,128)(2,1)S(1)} %get-tuple-element.10), kind=kOutput, calls=%fused_computation.8 | convolution fusion | flops 1260257280 | bytes 6062080 | tf_op jit(solution)/shard_map/dot_general | solution.py:16
  171.8 0.0 reduce-scatter.4.cloned.1.call-update
  171.8 0.2 reduce-scatter.6.cloned.1.call-start
  172.1 5.7 %convolution_convert_fusion.1 = bf16[2560,768]{1,0:T(8,128)(2,1)} fusion(bf16[320,2560]{1,0:T(8,128)(2,1)} %bitcast.76, bf16[320,768]{1,0:T(8,128)(2,1)} %get-tuple-element.9), kind=kOutput, calls=%fused_computation.7 | convolution fusion | flops 1260257280 | bytes 6062080 | tf_op jit(solution)/shard_map/dot_general | solution.py:16
  177.7 0.0 reduce-scatter.6.cloned.1.call-update
  177.7 0.0 reduce-scatter.8.cloned.1.call-start
  177.8 5.2 %convolution_convert_fusion = bf16[2560,768]{1,0:T(8,128)(2,1)} fusion(bf16[320,2560]{1,0:T(8,128)(2,1)S(1)} %bitcast.73, bf16[320,768]{1,0:T(8,128)(2,1)} %get-tuple-element.11), kind=kOutput, calls=%fused_computation.6 | convolution fusion | flops 1260257280 | bytes 6062080 | tf_op jit(solution)/shard_map/dot_general | solution.py:16
  183.0 0.0 reduce-scatter.8.cloned.1.call-update
  183.1 1.0 copy-done.7
  184.1 5.0 %convolution_convert_fusion.3 = bf16[320,2560]{1,0:T(8,128)(2,1)} fusion(bf16[320,768]{1,0:T(8,128)(2,1)S(1)} %copy-done.7, bf16[1,2560,768]{2,1,0:T(8,128)(2,1)} %all-gather.8.cloned.1.call-done), kind=kOutput, calls=%fused_computation.11 | convolution fusion | flops 1259110400 | bytes 6062080 | tf_op jit(solution)/shard_map/dot_general | solution.py:10
  189.1 3.7 all-to-all-start.1
  192.8 0.0 copy-start.5
  192.8 0.0 copy-start.6
  192.8 3.7 fusion.7
  196.6 0.0 copy-done.5
  196.6 2.7 fusion
  199.2 14.1 %all-to-all-done.1 = bf16[2,160,2560]{2,1,0:T(8,128)(2,1)S(1)} async-done(((bf16[2,160,2560]{2,1,0:T(8,128)(2,1)}), bf16[2,160,2560]{2,1,0:T(8,128)(2,1)S(1)}, u32[]{:S(2)}, u32[]{:S(2)}) %all-to-all-start.1) | async-done | bytes 1638432 | tf_op jit(solution)/shard_map/all_to_all | solution.py:70
  213.4 4.8 %all-to-all-start.3 = ((bf16[2,160,2560]{2,1,0:T(8,128)(2,1)}), bf16[2,160,2560]{2,1,0:T(8,128)(2,1)}, u32[]{:S(2)}, u32[]{:S(2)}) async-start(bf16[2,160,2560]{2,1,0:T(8,128)(2,1)} %bitcast.78), calls=%async_computation.3 | async-start | bytes 3276800 | tf_op jit(solution)/shard_map/all_to_all | solution.py:88
  218.2 2.5 gather_fusion.1
  220.7 17.3 %all-to-all-done.3 = bf16[2,160,2560]{2,1,0:T(8,128)(2,1)} async-done(((bf16[2,160,2560]{2,1,0:T(8,128)(2,1)}), bf16[2,160,2560]{2,1,0:T(8,128)(2,1)}, u32[]{:S(2)}, u32[]{:S(2)}) %all-to-all-start.3) | async-done | bytes 1638432 | tf_op jit(solution)/shard_map/all_to_all | solution.py:88
  238.0 4.4 %gather_fusion.3 = bf16[256,2560]{1,0:T(8,128)(2,1)S(1)} fusion(bf16[320,2560]{1,0:T(8,128)(2,1)} %bitcast.16, s32[1024]{0:T(1024)S(1)} %pad_clamp_fusion), kind=kCustom, calls=%fused_computation.3.clone | custom fusion | bytes 2622464 | tf_op jit(solution)/shard_map/jit(_take)/gather | solution.py:95
  242.4 0.0 copy-start.2
  242.4 1.2 broadcast_select_fusion
  243.7 0.5 copy-done.2
  244.2 1.4 multiply_convert_fusion.1
  245.6 1.8 bitcast_convert_fusion.2
  247.4 67.6 %reduce-scatter.6.cloned.1.call-done = bf16[160,768]{1,0:T(8,128)(2,1)} async-done(((bf16[2560,768]{1,0:T(8,128)(2,1)}), bf16[160,768]{1,0:T(8,128)(2,1)}) %reduce-scatter.6.cloned.1.call-update) | async-done | bytes 245776 | tf_op jit(solution)/shard_map/reduce_scatter | solution.py:101
  315.0 1.8 bitcast_convert_fusion.1
  316.8 71.4 %reduce-scatter.8.cloned.1.call-done = bf16[160,768]{1,0:T(8,128)(2,1)} async-done(((bf16[2560,768]{1,0:T(8,128)(2,1)}), bf16[160,768]{1,0:T(8,128)(2,1)}) %reduce-scatter.8.cloned.1.call-update) | async-done | bytes 245776 | tf_op jit(solution)/shard_map/reduce_scatter | solution.py:102
  388.2 1.8 bitcast_convert_fusion
  (14 shorter events, 0.1 us)
Async XLA Ops:
  7.2 12.3 %copy-start = (bf16[256,2560]{1,0:T(8,128)(2,1)S(1)}, bf16[256,2560]{1,0:T(8,128)(2,1)}, u32[]{:S(2)}) copy-start(bf16[256,2560]{1,0:T(8,128)(2,1)} %param.11) | copy-start | bytes 3932164
  7.2 54.6 %all-gather.4.cloned.1.call-start = ((), (), s32[]{:S(2)}) async-start(), calls=%async_computation.7 | async-start | bytes 4177920 | tf_op jit(solution)/shard_map/all_gather | solution.py:50
  7.9 104.1 %all-gather.6.cloned.1.call-start = ((), (), s32[]{:S(2)}) async-start(), calls=%async_computation.8 | async-start | bytes 4177920 | tf_op jit(solution)/shard_map/all_gather | solution.py:51
  8.7 153.5 %all-gather.8.cloned.1.call-start = ((), (), s32[]{:S(2)}) async-start(), calls=%async_computation.9 | async-start | bytes 4177920 | tf_op jit(solution)/shard_map/all_gather | solution.py:52
  19.5 5.4 %copy-start.1 = (bf16[320,2560]{1,0:T(8,128)(2,1)S(1)}, bf16[320,2560]{1,0:T(8,128)(2,1)}, u32[]{:S(2)}) copy-start(bf16[320,2560]{1,0:T(8,128)(2,1)} %gather_fusion.2) | copy-start | bytes 4915204
  52.6 64.4 %all-to-all-start.2 = ((bf16[2,160,2560]{2,1,0:T(8,128)(2,1)}), bf16[2,160,2560]{2,1,0:T(8,128)(2,1)S(1)}, u32[]{:S(2)}, u32[]{:S(2)}) async-start(bf16[2,160,2560]{2,1,0:T(8,128)(2,1)} %bitcast.13), calls=%async_computation.2 | async-start | bytes 3276800 | tf_op jit(solution)/shard_map/all_to_all | solution.py:77
  56.3 189.3 %reduce-scatter.4.cloned.1.call-start = ((), (), s32[]{:S(2)}) async-start(), calls=%async_computation.10 | async-start | bytes 4177920 | tf_op jit(solution)/shard_map/reduce_scatter | solution.py:100
  162.2 5.4 %copy-start.3 = (bf16[2,160,2560]{2,1,0:T(8,128)(2,1)S(1)}, bf16[2,160,2560]{2,1,0:T(8,128)(2,1)}, u32[]{:S(2)}) copy-start(bf16[2,160,2560]{2,1,0:T(8,128)(2,1)} %all_to_all.20) | copy-start | bytes 4915204
  171.8 143.2 %reduce-scatter.6.cloned.1.call-start = ((), (), s32[]{:S(2)}) async-start(), calls=%async_computation.11 | async-start | bytes 4177920 | tf_op jit(solution)/shard_map/reduce_scatter | solution.py:101
  177.7 210.5 %reduce-scatter.8.cloned.1.call-start = ((), (), s32[]{:S(2)}) async-start(), calls=%async_computation.12 | async-start | bytes 4177920 | tf_op jit(solution)/shard_map/reduce_scatter | solution.py:102
  183.0 1.1 copy-start.7
  189.1 24.3 %all-to-all-start.1 = ((bf16[2,160,2560]{2,1,0:T(8,128)(2,1)}), bf16[2,160,2560]{2,1,0:T(8,128)(2,1)S(1)}, u32[]{:S(2)}, u32[]{:S(2)}) async-start(bf16[2,160,2560]{2,1,0:T(8,128)(2,1)} %bitcast.79), calls=%async_computation.1 | async-start | bytes 3276800 | tf_op jit(solution)/shard_map/all_to_all | solution.py:70
  192.8 3.8 copy-start.5
  192.8 3.8 copy-start.6
  213.4 4.8 %copy-start.4 = (s32[256,1]{0,1:T(1,128)S(1)}, s32[256,1]{0,1:T(1,128)}, u32[]{:S(2)}) copy-start(s32[256,1]{0,1:T(1,128)} %param.12) | copy-start | bytes 3076
  213.4 24.6 %all-to-all-start.3 = ((bf16[2,160,2560]{2,1,0:T(8,128)(2,1)}), bf16[2,160,2560]{2,1,0:T(8,128)(2,1)}, u32[]{:S(2)}, u32[]{:S(2)}) async-start(bf16[2,160,2560]{2,1,0:T(8,128)(2,1)} %bitcast.78), calls=%async_computation.3 | async-start | bytes 3276800 | tf_op jit(solution)/shard_map/all_to_all | solution.py:88
  242.4 1.8 copy-start.2
Sparse Core Ops, SparseCore 0:
  10.3 51.4 all-gather.3
  64.1 47.8 all-gather.5
  114.3 47.8 all-gather.7
  172.0 69.5 reduce-scatter.3
  245.8 69.1 reduce-scatter.5
  318.8 69.4 reduce-scatter.7
where the time goes:
time: 398 us; the launch traced here: 397 us
  waiting for transfers between devices  269 us (68%)
  matrix products  41.8 us (11%)
  blocking collectives  24.7 us (6%)
  local copies, waits for them, and re-layouts  18.6 us (5%)
  other arithmetic  16.2 us (4%)
  between operations  14.3 us (4%)
  starting transfers between devices  12.6 us (3%)
    reduce_scatter x1, waiting for transfers between devices, shards(): lax.psum_scatter(part_down, 'dp', scatter_dimension=0, tiled=True)  71.4 us
    reduce_scatter x1, waiting for transfers between devices, shards(): lax.psum_scatter(part_up, 'dp', scatter_dimension=0, tiled=True)  67.6 us
    all_gather x1, waiting for transfers between devices, shards(): lax.all_gather(w_down, 'dp', axis=1, tiled=True)  45.2 us
    all_gather x1, waiting for transfers between devices, shards(): lax.all_gather(w_up, 'dp', axis=1, tiled=True)  45.2 us
    all_to_all x1, blocking collectives, shards(): lax.all_to_all(pack_rows(tokens), 'expert', split_axis=0, concat_axis=0,...  24.7 us
    all_to_all x1, waiting for transfers between devices, shards(): lax.all_to_all(token_grad.reshape(experts, capacity, model_width), 'exper...  17.3 us
    dot_general x3, matrix products, contract_first(): lax.dot_general(matrix_a, matrix_b, (((0,), (0,)), ((), ())), preferred_e...  15.1 us
    all_to_all x1, waiting for transfers between devices, shards(): lax.all_to_all(expert_out, 'expert', split_axis=0, concat_axis=0, tiled=T...  14.1 us
  transfers between devices with their start and end apart: 9, of which 7 were waited for; matrix products, arithmetic and copies ran while one was open for 16% of the time, Pallas kernels for 0%

commit v1 on v0

v1 whole, which is shorter than its diff:
```python
import functools

import jax
import jax.numpy as jnp
from jax import lax
from jax.experimental import pallas as pl
from jax.experimental.pallas import tpu as pltpu
from jax.sharding import PartitionSpec as P

TOP = 1
MESH = pl.DeviceIdType.MESH
VMEM_LIMIT = 58 * 1024 * 1024


def contract_last(matrix_a, matrix_b):
    return lax.dot_general(
        matrix_a, matrix_b, (((1,), (1,)), ((), ())), preferred_element_type=jnp.float32
    )


def contract_first(matrix_a, matrix_b):
    return lax.dot_general(
        matrix_a, matrix_b, (((0,), (0,)), ((), ())), preferred_element_type=jnp.float32
    )


class Sent:
    def __init__(self):
        self.made = []

    def start(self, make, cond=None):
        self.made.append((make, cond))
        run(lambda: make().start(), cond)

    def finish(self):
        for make, cond in self.made:
            run(lambda make=make: make().wait_send(), cond)


def run(body, cond=None):
    if cond is None:
        body()
    else:
        pl.when(cond)(body)


def places(lines, cross):
    dp = lax.axis_index("dp")
    return dp, lax.axis_index("expert"), dp // (2 * cross), (dp // 2) % cross, dp % 2


def greet(lines, cross, experts):
    dp, own, z, x, c = places(lines, cross)
    barrier = pltpu.get_barrier_semaphore()

    def hello(to_dp, to_expert):
        pl.semaphore_signal(barrier, inc=1, device_id=(to_dp, to_expert), device_id_type=MESH)

    run(lambda: hello(dp + 2 * cross, own), z < lines - 1)
    run(lambda: hello(dp - 2 * cross, own), z > 0)
    for o in range(1, cross):
        hello((z * cross + (x + o) % cross) * 2 + c, own)
    hello(dp + 1 - 2 * c, own)
    for o in range(1, experts):
        hello(dp, (own + o) % experts)
    up = jnp.where(z < lines - 1, 1, 0)
    down = jnp.where(z > 0, 1, 0)
    pl.semaphore_wait(barrier, up + down + (cross - 1) + 1 + (experts - 1))


def gather_kernel(lines, cross, experts, *refs):
    shards, blocks, fulls, landed = refs[0:3], refs[3:5], refs[5:8], refs[8:10]
    z_send, z_recv, x_send, x_recv, c_send, c_recv, y_send, y_recv, own_sem = refs[10:]
    dp, own, z, x, c = places(lines, cross)
    greet(lines, cross, experts)
    sent = Sent()
    local = []

    def at(q, r, s):
        return (q * cross + r) * 2 + s

    def copy(src, dst, send, recv, to_dp, to_expert):
        return pltpu.make_async_remote_copy(
            src_ref=src, dst_ref=dst, send_sem=send, recv_sem=recv,
            device_id=(to_dp, to_expert), device_id_type=MESH,
        )

    def y_copy(t, o):
        to = (own + o) % experts
        return copy(blocks[t].at[to], landed[t].at[own], y_send.at[t, o], y_recv.at[t, o], dp, to)

    def z_copy(k, q, step, src):
        side = 0 if step > 0 else 1
        return copy(src, fulls[k].at[at(q, x, c)], z_send.at[side, q, k], z_recv.at[q, k],
                    at(z + step, x, c), own)

    def x_copy(k, q, o, src):
        return copy(src, fulls[k].at[at(q, x, c)], x_send.at[q, o, k], x_recv.at[q, o, k],
                    at(z, (x + o) % cross, c), own)

    def c_copy(k, q, r, src):
        return copy(src, fulls[k].at[at(q, r, c)], c_send.at[q, r, k], c_recv.at[q, r, k],
                    at(z, x, 1 - c), own)

    bind = functools.partial
    for k in range(3):
        sent.start(bind(lambda k: z_copy(k, z, 1, shards[k]), k), z < lines - 1)
        sent.start(bind(lambda k: z_copy(k, z, -1, shards[k]), k), z > 0)
        for o in range(1, cross):
            sent.start(bind(lambda k, o: x_copy(k, z, o, shards[k]), k, o))
        sent.start(bind(lambda k: c_copy(k, z, x, shards[k]), k))
        if k == 0:
            for o in range(1, experts):
                sent.start(bind(lambda o: y_copy(0, o), o))
    for t in range(1, 2):
        for o in range(1, experts):
            sent.start(functools.partial(y_copy, t, o))
    for k in range(3):
        local.append(pltpu.make_async_copy(shards[k], fulls[k].at[dp], own_sem.at[k]))
    for t in range(2):
        local.append(pltpu.make_async_copy(blocks[t].at[own], landed[t].at[own], own_sem.at[3 + t]))
    for each in local:
        each.start()

    def from_z(k, q, step, cond):
        held = lambda: fulls[k].at[at(q, x, c)]
        run(lambda: z_copy(k, q, step, held()).wait_recv(), cond)
        onward = (z < lines - 1) if step > 0 else (z > 0)
        sent.start(lambda: z_copy(k, q, step, held()), cond & onward)
        for o in range(1, cross):
            sent.start(bind(lambda o: x_copy(k, q, o, held()), o), cond)
        sent.start(lambda: c_copy(k, q, x, held()), cond)

    def from_x(k, q, cond):
        for o in range(1, cross):
            r = (x - o + cross) % cross
            held = bind(lambda r: fulls[k].at[at(q, r, c)], r)
            run(lambda: copy(held(), held(), x_send.at[q, o, k], x_recv.at[q, o, k], dp + 1 - 2 * c, own).wait_recv(), cond)
            sent.start(bind(lambda r, held: c_copy(k, q, r, held()), r, held), cond)

    for s in range(1, lines + 1):
        for k in range(3):
            if s < lines:
                from_z(k, z - s, 1, z >= s)
                from_z(k, z + s, -1, z + s < lines)
            if s == 1:
                from_x(k, z, None)
            else:
                from_x(k, z - (s - 1), z >= s - 1)
                from_x(k, z + (s - 1), z + s - 1 < lines)
    for k in range(3):
        for q in range(lines):
            for r in range(cross):
                held = fulls[k].at[at(q, r, 1 - c)]
                copy(held, held, c_send.at[q, r, k], c_recv.at[q, r, k], dp + 1 - 2 * c, own).wait_recv()
    for t in range(2):
        for o in range(1, experts):
            held = landed[t].at[(own - o + experts) % experts]
            copy(held, held, y_send.at[t, o], y_recv.at[t, o], dp, (own + o) % experts).wait_recv()
    for each in local:
        each.wait()
    sent.finish()


def scatter_kernel(lines, cross, experts, *refs):
    parts, blocks, totals, landed = refs[0:3], refs[3:5], refs[5:8], refs[8:10]
    c_buf, x_buf, z_buf, stage = refs[10:14]
    z_send, z_recv, x_send, x_recv, c_send, c_recv, y_send, y_recv, own_sem = refs[14:]
    dp, own, z, x, c = places(lines, cross)
    greet(lines, cross, experts)
    sent = Sent()
    bind = functools.partial

    def at(q, r, s):
        return (q * cross + r) * 2 + s

    def copy(src, dst, send, recv, to_dp, to_expert):
        return pltpu.make_async_remote_copy(
            src_ref=src, dst_ref=dst, send_sem=send, recv_sem=recv,
            device_id=(to_dp, to_expert), device_id_type=MESH,
        )

    def y_copy(t, o):
        to = (own + o) % experts
        return copy(blocks[t].at[to], landed[t].at[own], y_send.at[t, o], y_recv.at[t, o], dp, to)

    def c_copy(k, q, r):
        return copy(parts[k].at[at(q, r, 1 - c)], c_buf.at[k, q, r], c_send.at[k, q, r],
                    c_recv.at[k, q, r], dp + 1 - 2 * c, own)

    def x_copy(k, q, o):
        to = (x + o) % cross
        return copy(c_buf.at[k, q, to], x_buf.at[k, q, o], x_send.at[k, q, o],
                    x_recv.at[k, q, o], at(z, to, c), own)

    def z_copy(k, q, step):
        side = 0 if step > 0 else 1
        return copy(stage.at[k, q], z_buf.at[side, k, q], z_send.at[side, k, q],
                    z_recv.at[side, k, q], at(z + step, x, c), own)

    order = []
    for d in range(lines - 1, 0, -1):
        order.append((d, z + d, z + d < lines))
        order.append((-d, z - d, z >= d))
    order.append((0, z, None))

    for t in range(2):
        for o in range(1, experts):
            sent.start(bind(y_copy, t, o))
    local = []
    for t in range(2):
        local.append(pltpu.make_async_copy(blocks[t].at[own], landed[t].at[own], own_sem.at[t]))
    for each in local:
        each.start()
    for d, q, cond in order:
        for k in range(3):
            for o in range(cross):
                sent.start(bind(lambda k, q, o: c_copy(k, q, (x + 1 + o) % cross), k, q, o), cond)

    def pair(k, q, r):
        c_copy(k, q, r).wait_recv()
        return parts[k][at(q, r, c)].astype(jnp.float32) + c_buf[k, q, r].astype(jnp.float32)

    for d, q, cond in order:
        for k in range(3):
            for o in range(1, cross):
                def body(k=k, q=q, o=o):
                    r = (x + o) % cross
                    c_buf[k, q, r] = pair(k, q, r).astype(jnp.bfloat16)
                run(body, cond)
                sent.start(bind(x_copy, k, q, o), cond)

    for d, q, cond in order:
        for k in range(3):
            def body(k=k, q=q, d=d):
                total = pair(k, q, x)
                for o in range(1, cross):
                    x_copy(k, q, o).wait_recv()
                    total = total + x_buf[k, q, o].astype(jnp.float32)
                if d == 0:
                    totals[k][...] = total
                else:
                    stage[k, q] = total.astype(jnp.bfloat16)
            run(body, cond)
            if d >= 0:
                def rest(k=k, q=q, d=d):
                    z_copy(k, q, 1).wait_recv()
                    more = z_buf[0, k, q].astype(jnp.float32)
                    if d == 0:
                        totals[k][...] += more
                    else:
                        stage[k, q] = (stage[k, q].astype(jnp.float32) + more).astype(jnp.bfloat16)
                run(rest, (z > 0) if cond is None else cond & (z > 0))
            if d <= 0:
                def rest(k=k, q=q, d=d):
                    z_copy(k, q, -1).wait_recv()
                    more = z_buf[1, k, q].astype(jnp.float32)
                    if d == 0:
                        totals[k][...] += more
                    else:
                        stage[k, q] = (stage[k, q].astype(jnp.float32) + more).astype(jnp.bfloat16)
                run(rest, (z < lines - 1) if cond is None else cond & (z < lines - 1))
            if d != 0:
                sent.start(bind(z_copy, k, q, 1 if d > 0 else -1), cond)
    for t in range(2):
        for o in range(1, experts):
            held = landed[t].at[(own - o + experts) % experts]
            copy(held, held, y_send.at[t, o], y_recv.at[t, o], dp, (own + o) % experts).wait_recv()
    for each in local:
        each.wait()
    sent.finish()


def semaphores(lines, cross, experts, own):
    dma = pltpu.SemaphoreType.DMA
    return dma, [dma((2, experts)), dma((2, experts)), dma((own,))]


def gather_all(lines, cross, experts, trio, blocks):
    n = lines * cross * 2
    rows, width = trio[0].shape
    dma, last = semaphores(lines, cross, experts, 5)
    anywhere = pl.BlockSpec(memory_space=pl.ANY)
    full = jax.ShapeDtypeStruct((n, rows, width), jnp.bfloat16)
    outs = pl.pallas_call(
        functools.partial(gather_kernel, lines, cross, experts),
        out_shape=[full] * 3 + [jax.ShapeDtypeStruct(b.shape, b.dtype) for b in blocks],
        in_specs=[anywhere] * 5,
        out_specs=[anywhere] * 5,
        scratch_shapes=[dma((2, lines, 3)), dma((lines, 3))]
        + [dma((lines, cross, 3)) for _ in range(4)] + last,
        compiler_params=pltpu.CompilerParams(collective_id=0, has_side_effects=True),
        name="gather_and_exchange",
    )(*trio, *blocks)
    return [f.reshape(n * rows, width) for f in outs[:3]], outs[3:]


def scatter_all(lines, cross, experts, parts, blocks):
    n = lines * cross * 2
    width = parts[0].shape[1]
    rows = parts[0].shape[0] // n
    dma, last = semaphores(lines, cross, experts, 2)
    anywhere = pl.BlockSpec(memory_space=pl.ANY)
    inside = pl.BlockSpec(memory_space=pltpu.VMEM)
    total = jax.ShapeDtypeStruct((rows, width), jnp.float32)
    block = (rows, width)
    outs = pl.pallas_call(
        functools.partial(scatter_kernel, lines, cross, experts),
        out_shape=[total] * 3 + [jax.ShapeDtypeStruct(b.shape, b.dtype) for b in blocks],
        in_specs=[inside] * 3 + [anywhere] * 2,
        out_specs=[inside] * 3 + [anywhere] * 2,
        scratch_shapes=[
            pltpu.VMEM((3, lines, cross) + block, jnp.bfloat16),
            pltpu.VMEM((3, lines, cross) + block, jnp.bfloat16),
            pltpu.VMEM((2, 3, lines) + block, jnp.bfloat16),
            pltpu.VMEM((3, lines) + block, jnp.bfloat16),
            dma((2, 3, lines)), dma((2, 3, lines)),
        ] + [dma((3, lines, cross)) for _ in range(4)] + last,
        compiler_params=pltpu.CompilerParams(
            collective_id=1, has_side_effects=True, vmem_limit_bytes=VMEM_LIMIT
        ),
        name="scatter_and_return",
    )(*[p.reshape(n, rows, width) for p in parts], *blocks)
    return outs[:3], outs[3:]


def shards(lines, cross, tokens, routes, gate_levels, w_gate, w_up, w_down, grad_out):
    experts = lax.axis_size("expert")
    tok_rows = tokens.shape[0]
    model_width = tokens.shape[1]
    capacity = min(tok_rows, tok_rows * TOP * 5 // (4 * experts))
    slot_count = experts * capacity
    expert_of = routes[:, 0]
    onehot = (expert_of[:, None] == jnp.arange(experts, dtype=jnp.int32)[None, :]).astype(jnp.bfloat16)
    place = jnp.arange(tok_rows, dtype=jnp.int32)
    earlier = jnp.dot(
        (place[:, None] > place[None, :]).astype(jnp.bfloat16), onehot,
        preferred_element_type=jnp.float32,
    )
    slot_rank = jnp.sum(earlier * onehot.astype(jnp.float32), axis=1).astype(jnp.int32)
    slot_index = expert_of * capacity + slot_rank
    to_slot = (slot_index[:, None] == jnp.arange(slot_count, dtype=jnp.int32)[None, :]).astype(
        jnp.bfloat16
    )
    gate_weight = gate_levels.astype(jnp.float32) / 64.0

    def pack_rows(values):
        return contract_first(to_slot, values).astype(jnp.bfloat16).reshape(
            experts, capacity, model_width
        )

    def unpack_rows(values):
        return jnp.dot(
            to_slot, values.reshape(slot_count, model_width), preferred_element_type=jnp.float32
        )

    out_grad = (gate_weight * grad_out.astype(jnp.float32)).astype(jnp.bfloat16)
    (gate_full, up_full, down_full), (received, grad_rows) = gather_all(
        lines, cross, experts, (w_gate[0], w_up[0], w_down[0]),
        (pack_rows(tokens), pack_rows(out_grad)),
    )
    received = received.reshape(slot_count, model_width)
    grad_rows = grad_rows.reshape(slot_count, model_width)
    act_gate = jnp.dot(received, gate_full, preferred_element_type=jnp.float32)
    act_up = jnp.dot(received, up_full, preferred_element_type=jnp.float32)
    sigmoid_gate = jax.nn.sigmoid(act_gate)
    silu_gate = act_gate * sigmoid_gate
    hidden = (silu_gate * act_up).astype(jnp.bfloat16)
    expert_out = contract_last(hidden, down_full).astype(jnp.bfloat16)
    hidden_grad = jnp.dot(grad_rows, down_full, preferred_element_type=jnp.float32)
    gate_delta = (
        hidden_grad * act_up * sigmoid_gate * (1.0 + act_gate * (1.0 - sigmoid_gate))
    ).astype(jnp.bfloat16)
    up_delta = (hidden_grad * silu_gate).astype(jnp.bfloat16)
    token_grad = (contract_last(gate_delta, gate_full) + contract_last(up_delta, up_full)).astype(
        jnp.bfloat16
    )
    part_gate = contract_first(received, gate_delta).astype(jnp.bfloat16)
    part_up = contract_first(received, up_delta).astype(jnp.bfloat16)
    part_down = contract_first(grad_rows, hidden).astype(jnp.bfloat16)
    (grad_gate, grad_up, grad_down), (returned, arrived) = scatter_all(
        lines, cross, experts, (part_gate, part_up, part_down),
        (expert_out.reshape(experts, capacity, model_width),
         token_grad.reshape(experts, capacity, model_width)),
    )
    moe_out = (gate_weight * unpack_rows(returned)).astype(jnp.bfloat16)
    grad_tokens = unpack_rows(arrived).astype(jnp.bfloat16)
    return (moe_out, grad_tokens, grad_gate[None], grad_up[None], grad_down[None])


def solution(mesh):
    chips = mesh.shape["dp"] // 2
    lines = 4 if chips % 4 == 0 else chips
    in_specs = (
        P(("dp", "expert"), None),
        P(("dp", "expert"), None),
        P(("dp", "expert"), None),
        P("expert", "dp", None),
        P("expert", "dp", None),
        P("expert", "dp", None),
        P(("dp", "expert"), None),
    )
    out_specs = (
        P(("dp", "expert"), None),
        P(("dp", "expert"), None),
        P("expert", "dp", None),
        P("expert", "dp", None),
        P("expert", "dp", None),
    )
    return jax.shard_map(
        functools.partial(shards, lines, chips // lines),
        mesh=mesh, in_specs=in_specs, out_specs=out_specs, check_vma=False,
    )
```

time: 398 us -> 196 us (0.49)
  waiting for transfers between devices: 269 us -> 0 us
  Pallas kernels: 0 us -> 152 us
  blocking collectives: 24.7 us -> 0 us
  local copies, waits for them, and re-layouts: 18.6 us -> 3.1 us
  other arithmetic: 16.2 us -> 1.48 us
  between operations: 14.3 us -> 0.75 us
  starting transfers between devices: 12.6 us -> 0 us
    pallas_call x0 -> x2, Pallas kernels: none -> 152 us  [the longest x1 77.5 us: gather_all(): pl.pallas_call(functools.partial(gather_kernel, lines, cross, experts), o...]
    reduce_scatter x3 -> x0, waiting for transfers between devices: 139 us -> none  [the longest x1 71.4 us: shards(): lax.psum_scatter(part_down, 'dp', scatter_dimension=0, tiled=True)]
    all_gather x3 -> x0, waiting for transfers between devices: 95.9 us -> none  [the longest x1 45.2 us: shards(): lax.all_gather(w_down, 'dp', axis=1, tiled=True)]
    all_to_all x3 -> x0, waiting for transfers between devices: 31.4 us -> none  [the longest x1 17.3 us: shards(): lax.all_to_all(token_grad.reshape(experts, capacity, model_width), 'exper...]
    all_to_all x1 -> x0, blocking collectives: 24.7 us -> none  [shards(): lax.all_to_all(pack_rows(tokens), 'expert', split_axis=0, concat_axis=0,...]
    gather x4 -> x0, local copies, waits for them, and re-layouts: 13.3 us -> none  [the longest x2 6.4 us: pack_rows(): jnp.take(values, source_row, axis=0) * filled]
    all_to_all x3 -> x0, starting transfers between devices: 12.2 us -> none  [the longest x1 4.8 us: shards(): lax.all_to_all(token_grad.reshape(experts, capacity, model_width), 'exper...]
    dot_general x0 -> x3, matrix products: none -> 6.41 us  [the longest x2 5.46 us: unpack_rows(): jnp.dot(to_slot, values.reshape(slot_count, model_width), preferred_eleme...]
  transfers between devices with their start and end apart: 9 -> 0, of which waited for: 7 -> 0; matrix products, arithmetic and copies ran while one was open for 16% -> 0% of each run, Pallas kernels for 0% -> 0%
where the time goes in v1:
time: 196 us
  Pallas kernels  152 us (78%)
  matrix products  38.4 us (20%)
  local copies, waits for them, and re-layouts  3.1 us (2%)
    pallas_call x1, Pallas kernels, gather_all(): pl.pallas_call(functools.partial(gather_kernel, lines, cross, experts), o...  77.5 us
    pallas_call x1, Pallas kernels, scatter_all(): pl.pallas_call(functools.partial(scatter_kernel, lines, cross, experts),...  74.8 us
    dot_general x5, matrix products, contract_first(): lax.dot_general(matrix_a, matrix_b, (((0,), (0,)), ((), ())), preferred_e...  17.9 us
    dot_general x3, matrix products, contract_last(): lax.dot_general(matrix_a, matrix_b, (((1,), (1,)), ((), ())), preferred_e...  6.83 us
    dot_general x2, matrix products, unpack_rows(): jnp.dot(to_slot, values.reshape(slot_count, model_width), preferred_eleme...  5.46 us
    dot_general x1, matrix products, shards(): jnp.dot(grad_rows, down_full, preferred_element_type=jnp.float32)  4.18 us

profile of v1, /device:TPU:0, one launch (start us, length us, event | category | flops | bytes accessed | tf_op | source)
XLA Modules:
  0.0 196.0 jit_solution(11220031520811138170)
XLA Ops:
  0.6 0.0 copy-start
  0.6 0.8 convert_multiply_fusion
  1.4 0.9 fusion.3
  2.4 0.7 multiply_add_fusion
  3.1 3.2 %convolution_convert_fusion.4 = bf16[320,2560]{1,0:T(8,128)(2,1)} fusion(bf16[256,2560]{1,0:T(8,128)(2,1)} %param.13, f32[256]{0:T(256)S(1)} %bitcast.63, s32[256]{0:T(256)S(1)} %bitcast.59), kind=kOutput, calls=%fused_computation.7 | convolution fusion | flops 422297600 | bytes 2951168 | tf_op jit(solution)/shard_map/dot_general | solution.py:22
  6.3 0.0 copy-done
  6.3 2.0 %convolution_convert_fusion.5 = bf16[320,2560]{1,0:T(8,128)(2,1)} fusion(bf16[256,2560]{1,0:T(8,128)(2,1)S(1)} %copy-done, s32[256]{0:T(256)S(1)} %bitcast.60), kind=kOutput, calls=%fused_computation.8 | convolution fusion | flops 420331520 | bytes 2950144 | tf_op jit(solution)/shard_map/dot_general | solution.py:22
  8.3 77.5 %gather_and_exchange.1 = (bf16[16,160,768]{2,1,0:T(8,128)(2,1)}, bf16[16,160,768]{2,1,0:T(8,128)(2,1)}, bf16[16,160,768]{2,1,0:T(8,128)(2,1)}, bf16[2,160,2560]{2,1,0:T(8,128)(2,1)}, bf16[2,160,2560]{2,1,0:T(8,128)(2,1)}) custom-call(bf16[160,768]{1,0:T(8,128)(2,1)} %bitcast.56, bf16[160,768]{1,0:T(8,128)(2,1)} %bitcast.57, bf16[160,768]{1,0:T(8,128)(2,1)} %bitcast.58, ...), custom_call_target="tpu_custom_call" | custom-call | tf_op jit(solution)/shard_map/gather_and_exchange/pallas_call | solution.py:285
  85.8 0.0 copy-start.7
  85.8 0.0 copy-start.8
  85.8 4.2 %fusion.11 = f32[320,768]{1,0:T(8,128)S(1)} fusion(bf16[320,2560]{1,0:T(8,128)(2,1)} %bitcast.77, bf16[2560,768]{1,0:T(8,128)(2,1)} %bitcast.67), kind=kOutput, calls=%fused_computation.31 | convolution fusion | flops 1258291200 | bytes 6553600 | tf_op jit(solution)/shard_map/dot_general | solution.py:370
  90.0 0.0 copy-done.7
  90.0 0.0 copy-done.8
  90.0 0.0 copy-start.6
  90.0 1.4 fusion.12
  91.5 0.7 copy-done.6
  92.2 1.7 multiply_convert_fusion.2
  93.8 1.5 fusion.13
  95.3 0.0 copy-start.5
  95.3 2.7 %fusion = bf16[320,2560]{1,0:T(8,128)(2,1)} fusion(f32[320,2560]{1,0:T(8,128)S(1)} %fusion.13, bf16[320,768]{1,0:T(8,128)(2,1)S(1)} %get-tuple-element.27, bf16[2560,768]{1,0:T(8,128)(2,1)S(1)} %bitcast.70), kind=kOutput, calls=%fused_computation.5 | convolution fusion | flops 1259929600 | bytes 9338880 | tf_op jit(solution)/shard_map/dot_general | solution.py:16
  98.1 0.0 copy-done.5
  98.1 0.0 copy-start.9
  98.1 2.6 %convolution_convert_fusion.3 = bf16[320,2560]{1,0:T(8,128)(2,1)} fusion(bf16[320,768]{1,0:T(8,128)(2,1)S(1)} %get-tuple-element.25, bf16[2560,768]{1,0:T(8,128)(2,1)S(1)} %bitcast.68), kind=kOutput, calls=%fused_computation.6 | convolution fusion | flops 1259110400 | bytes 6062080 | tf_op jit(solution)/shard_map/dot_general | solution.py:16
  100.7 0.0 copy-done.9
  100.7 4.2 %convolution_convert_fusion = bf16[2560,768]{1,0:T(8,128)(2,1)} fusion(bf16[320,2560]{1,0:T(8,128)(2,1)S(1)} %bitcast.78, bf16[320,768]{1,0:T(8,128)(2,1)S(1)} %get-tuple-element.25), kind=kOutput, calls=%fused_computation | convolution fusion | flops 1260257280 | bytes 6062080 | tf_op jit(solution)/shard_map/dot_general | solution.py:22
  104.9 4.3 %convolution_convert_fusion.2 = bf16[2560,768]{1,0:T(8,128)(2,1)} fusion(bf16[320,2560]{1,0:T(8,128)(2,1)S(1)} %bitcast.75, bf16[320,768]{1,0:T(8,128)(2,1)S(1)} %get-tuple-element.26), kind=kOutput, calls=%fused_computation.2 | convolution fusion | flops 1260257280 | bytes 6062080 | tf_op jit(solution)/shard_map/dot_general | solution.py:22
  109.2 4.1 %convolution_convert_fusion.1 = bf16[2560,768]{1,0:T(8,128)(2,1)} fusion(bf16[320,2560]{1,0:T(8,128)(2,1)S(1)} %bitcast.76, bf16[320,768]{1,0:T(8,128)(2,1)S(1)} %get-tuple-element.27), kind=kOutput, calls=%fused_computation.1 | convolution fusion | flops 1260257280 | bytes 6062080 | tf_op jit(solution)/shard_map/dot_general | solution.py:22
  113.4 74.8 %scatter_and_return.1 = (f32[160,768]{1,0:T(8,128)}, f32[160,768]{1,0:T(8,128)}, f32[160,768]{1,0:T(8,128)}, bf16[2,160,2560]{2,1,0:T(8,128)(2,1)}, bf16[2,160,2560]{2,1,0:T(8,128)(2,1)}) custom-call(bf16[16,160,768]{2,1,0:T(8,128)(2,1)} %bitcast.48, bf16[16,160,768]{2,1,0:T(8,128)(2,1)} %bitcast.49, bf16[16,160,768]{2,1,0:T(8,128)(2,1)} %bitcast.47, ...), custom_call_target="tpu_custom_call" | custom-call | tf_op jit(solution)/shard_map/scatter_and_return/pallas_call | solution.py:307
  188.2 0.0 copy-start.1
  188.2 3.5 %fusion.1 = bf16[256,2560]{1,0:T(8,128)(2,1)} fusion(bf16[320,2560]{1,0:T(8,128)(2,1)} %bitcast.79, f32[256]{0:T(256)S(1)} %bitcast.64, s32[256]{0:T(256)S(1)} %bitcast.61), kind=kOutput, calls=%fused_computation.9 | convolution fusion | flops 420823040 | bytes 2951168 | tf_op jit(solution)/shard_map/dot_general | solution.py:353
  191.7 0.0 copy-start.4
  191.7 0.0 copy-done.1
  191.7 0.0 copy-start.3
  191.7 2.0 convolution_convert_fusion.6
  193.7 0.0 copy-done.4
  193.7 0.0 copy-start.2
  193.7 0.8 copy.15
  194.5 0.0 copy-done.3
  194.5 0.8 copy.16
  195.2 0.0 copy-done.2
  195.2 0.8 copy.17
  (1 shorter events, 0.0 us)
Async XLA Ops:
  0.6 5.7 %copy-start = (bf16[256,2560]{1,0:T(8,128)(2,1)S(1)}, bf16[256,2560]{1,0:T(8,128)(2,1)}, u32[]{:S(2)}) copy-start(bf16[256,2560]{1,0:T(8,128)(2,1)} %param.7) | copy-start | bytes 3932164
  85.8 4.2 %copy-start.7 = (bf16[16,160,768]{2,1,0:T(8,128)(2,1)S(1)}, bf16[16,160,768]{2,1,0:T(8,128)(2,1)}, u32[]{:S(2)}) copy-start(bf16[16,160,768]{2,1,0:T(8,128)(2,1)} %get-tuple-element.19) | copy-start | bytes 11796484
  85.8 4.3 %copy-start.8 = (bf16[2,160,2560]{2,1,0:T(8,128)(2,1)S(1)}, bf16[2,160,2560]{2,1,0:T(8,128)(2,1)}, u32[]{:S(2)}) copy-start(bf16[2,160,2560]{2,1,0:T(8,128)(2,1)} %get-tuple-element.15) | copy-start | bytes 4915204
  90.0 2.1 %copy-start.6 = (bf16[16,160,768]{2,1,0:T(8,128)(2,1)S(1)}, bf16[16,160,768]{2,1,0:T(8,128)(2,1)}, u32[]{:S(2)}) copy-start(bf16[16,160,768]{2,1,0:T(8,128)(2,1)} %get-tuple-element.18) | copy-start | bytes 11796484
  95.3 2.7 %copy-start.5 = (bf16[16,160,768]{2,1,0:T(8,128)(2,1)S(1)}, bf16[16,160,768]{2,1,0:T(8,128)(2,1)}, u32[]{:S(2)}) copy-start(bf16[16,160,768]{2,1,0:T(8,128)(2,1)} %get-tuple-element.17) | copy-start | bytes 11796484
  98.1 2.6 %copy-start.9 = (bf16[2,160,2560]{2,1,0:T(8,128)(2,1)S(1)}, bf16[2,160,2560]{2,1,0:T(8,128)(2,1)}, u32[]{:S(2)}) copy-start(bf16[2,160,2560]{2,1,0:T(8,128)(2,1)} %get-tuple-element.16) | copy-start | bytes 4915204
  188.2 3.5 %copy-start.1 = (bf16[2,160,2560]{2,1,0:T(8,128)(2,1)S(1)}, bf16[2,160,2560]{2,1,0:T(8,128)(2,1)}, u32[]{:S(2)}) copy-start(bf16[2,160,2560]{2,1,0:T(8,128)(2,1)} %get-tuple-element.21) | copy-start | bytes 4915204
  191.7 2.0 %copy-start.4 = (f32[160,768]{1,0:T(8,128)S(1)}, f32[160,768]{1,0:T(8,128)}, u32[]{:S(2)}) copy-start(f32[160,768]{1,0:T(8,128)} %get-tuple-element.22) | copy-start | bytes 1474564
  191.7 2.7 %copy-start.3 = (f32[160,768]{1,0:T(8,128)S(1)}, f32[160,768]{1,0:T(8,128)}, u32[]{:S(2)}) copy-start(f32[160,768]{1,0:T(8,128)} %get-tuple-element.23) | copy-start | bytes 1474564
  193.7 1.6 copy-start.2

commit v2 on v0

v2 whole, which is shorter than its diff:
```python
import functools

import jax
import jax.numpy as jnp
from jax import lax
from jax.experimental import pallas as pl
from jax.experimental.pallas import tpu as pltpu
from jax.sharding import PartitionSpec as P

TOP = 1
MESH = pl.DeviceIdType.MESH
VMEM_LIMIT = 62 * 1024 * 1024


def contract_last(matrix_a, matrix_b):
    return lax.dot_general(
        matrix_a, matrix_b, (((1,), (1,)), ((), ())), preferred_element_type=jnp.float32
    )


def contract_first(matrix_a, matrix_b):
    return lax.dot_general(
        matrix_a, matrix_b, (((0,), (0,)), ((), ())), preferred_element_type=jnp.float32
    )


class Sent:
    def __init__(self):
        self.made = []

    def start(self, make, cond=None):
        self.made.append((make, cond))
        run(lambda: make().start(), cond)

    def finish(self):
        for make, cond in self.made:
            run(lambda make=make: make().wait_send(), cond)


def run(body, cond=None):
    if cond is None:
        body()
    else:
        pl.when(cond)(body)


def places(lines, cross):
    dp = lax.axis_index("dp")
    return dp, lax.axis_index("expert"), dp // (2 * cross), (dp // 2) % cross, dp % 2


def greet(lines, cross, experts):
    dp, own, z, x, c = places(lines, cross)
    barrier = pltpu.get_barrier_semaphore()

    def hello(to_dp, to_expert):
        pl.semaphore_signal(barrier, inc=1, device_id=(to_dp, to_expert), device_id_type=MESH)

    run(lambda: hello(dp + 2 * cross, own), z < lines - 1)
    run(lambda: hello(dp - 2 * cross, own), z > 0)
    for o in range(1, cross):
        hello((z * cross + (x + o) % cross) * 2 + c, own)
    hello(dp + 1 - 2 * c, own)
    for o in range(1, experts):
        hello(dp, (own + o) % experts)
    up = jnp.where(z < lines - 1, 1, 0)
    down = jnp.where(z > 0, 1, 0)
    pl.semaphore_wait(barrier, up + down + (cross - 1) + 1 + (experts - 1))


def layer_kernel(lines, cross, experts, *refs):
    shards, to_slot, tokens, levels, grad_out, totals = refs[0:3], refs[3], refs[4], refs[5], refs[6], refs[7]
    returned = refs[8:10]
    fulls, blocks, landed, outs, acts, deltas, parts, c_buf, x_buf, z_buf, acc = refs[10:21]
    (z_send, z_recv, x_send, x_recv, c_send, c_recv, y_send, y_recv, own_sem,
     rz_send, rz_recv, rx_send, rx_recv, rc_send, rc_recv, ry_send, ry_recv) = refs[21:]
    dp, own, z, x, c = places(lines, cross)
    other = dp + 1 - 2 * c
    per = 2 * cross
    rows, width = fulls.shape[2], fulls.shape[3]
    slots = acts.shape[1]
    capacity = slots // experts
    wide = per * rows
    f32, bf16 = jnp.float32, jnp.bfloat16
    bind = functools.partial
    sent = Sent()

    def at(q, r, s):
        return (q * cross + r) * 2 + s

    def lanes(q):
        return pl.ds(pl.multiple_of(q * wide, 128), wide)

    def copy(src, dst, send, recv, to_dp, to_expert):
        return pltpu.make_async_remote_copy(
            src_ref=src, dst_ref=dst, send_sem=send, recv_sem=recv,
            device_id=(to_dp, to_expert), device_id_type=MESH,
        )

    def y_copy(t, o):
        to = (own + o) % experts
        return copy(blocks.at[t, to], landed.at[t, own], y_send.at[t, o], y_recv.at[t, o], dp, to)

    def z_copy(k, q, step, src):
        side = 0 if step > 0 else 1
        return copy(src, fulls.at[k, at(q, x, c)], z_send.at[side, q, k], z_recv.at[q, k],
                    at(z + step, x, c), own)

    def x_copy(k, q, o, src):
        return copy(src, fulls.at[k, at(q, x, c)], x_send.at[q, o, k], x_recv.at[q, o, k],
                    at(z, (x + o) % cross, c), own)

    def c_copy(k, q, r, src):
        return copy(src, fulls.at[k, at(q, r, c)], c_send.at[q, r, k], c_recv.at[q, r, k],
                    other, own)

    greet(lines, cross, experts)
    for k in range(3):
        sent.start(bind(lambda k: z_copy(k, z, 1, shards[k]), k), z < lines - 1)
        sent.start(bind(lambda k: z_copy(k, z, -1, shards[k]), k), z > 0)
        for o in range(1, cross):
            sent.start(bind(lambda k, o: x_copy(k, z, o, shards[k]), k, o))
        sent.start(bind(lambda k: c_copy(k, z, x, shards[k]), k))
    local = [
        pltpu.make_async_copy(shards[k], fulls.at[k, dp], own_sem.at[k]) for k in range(3)
    ]
    for each in local:
        each.start()

    for t in range(2):
        def pack(q, carry, t=t):
            values = (tokens, grad_out)[t][:, lanes(q)]
            if t == 1:
                weight = levels[...].astype(f32) / 64.0
                values = (weight * values.astype(f32)).astype(bf16)
            packed = jnp.dot(to_slot[...], values, preferred_element_type=f32).astype(bf16)
            blocks[t, :, :, lanes(q)] = packed.reshape(experts, capacity, wide)
            return carry
        lax.fori_loop(0, lines, pack, 0)
        for o in range(1, experts):
            sent.start(bind(y_copy, t, o))
        landed[t, own] = blocks[t, own]
    for each in local:
        each.wait()

    def from_z(k, q, step, cond):
        held = lambda: fulls.at[k, at(q, x, c)]
        run(lambda: z_copy(k, q, step, held()).wait_recv(), cond)
        onward = (z < lines - 1) if step > 0 else (z > 0)
        sent.start(lambda: z_copy(k, q, step, held()), cond & onward)
        for o in range(1, cross):
            sent.start(bind(lambda o: x_copy(k, q, o, held()), o), cond)
        sent.start(lambda: c_copy(k, q, x, held()), cond)

    def from_x(k, q, cond):
        for o in range(1, cross):
            r = (x - o + cross) % cross
            held = bind(lambda r: fulls.at[k, at(q, r, c)], r)
            run(lambda: copy(held(), held(), x_send.at[q, o, k], x_recv.at[q, o, k], other, own).wait_recv(), cond)
            sent.start(bind(lambda r, held: c_copy(k, q, r, held()), r, held), cond)

    table = [sorted(range(lines), key=lambda q: (abs(q - p), q)) for p in range(lines)]

    def near(j):
        q = table[0][j]
        for p in range(1, lines):
            q = jnp.where(z == p, table[p][j], q)
        return q

    def slice_of(t, q):
        return landed[t, :, :, lanes(q)].reshape(slots, wide)

    def forward(j):
        q = near(j)
        for k in range(3):
            for r in range(cross):
                held = fulls.at[k, at(q, r, 1 - c)]
                copy(held, held, c_send.at[q, r, k], c_recv.at[q, r, k], other, own).wait_recv()
            weights = fulls[k, pl.ds(q * per, per)].reshape(wide, width)
            more = jnp.dot(slice_of(0 if k < 2 else 1, q), weights, preferred_element_type=f32)
            acts[k] = more if j == 0 else acts[k] + more

    done = 0
    for s in range(1, lines + 1):
        for k in range(3):
            if s < lines:
                from_z(k, z - s, 1, z >= s)
                from_z(k, z + s, -1, z + s < lines)
            if s == 1:
                from_x(k, z, None)
            else:
                from_x(k, z - (s - 1), z >= s - 1)
                from_x(k, z + (s - 1), z + s - 1 < lines)
        if s == max(1, lines // 2):
            for t in range(2):
                for o in range(1, experts):
                    held = landed.at[t, (own - o + experts) % experts]
                    copy(held, held, y_send.at[t, o], y_recv.at[t, o], dp, (own + o) % experts).wait_recv()
        if s >= max(1, lines // 2):
            last = {lines: lines, lines - 1: lines - 1}.get(s, s - 1)
            while done < last:
                forward(done)
                done += 1

    step_rows = 32

    def middle(b, carry):
        block = pl.ds(pl.multiple_of(b * step_rows, step_rows), step_rows)
        act_gate, act_up, hidden_grad = acts[0, block], acts[1, block], acts[2, block]
        sigmoid_gate = jax.nn.sigmoid(act_gate)
        silu_gate = act_gate * sigmoid_gate
        deltas[0, block] = (
            hidden_grad * act_up * sigmoid_gate * (1.0 + act_gate * (1.0 - sigmoid_gate))
        ).astype(bf16)
        deltas[1, block] = (hidden_grad * silu_gate).astype(bf16)
        deltas[2, block] = (silu_gate * act_up).astype(bf16)
        return carry

    lax.fori_loop(0, slots // step_rows, middle, 0)

    def ry_copy(t, o):
        to = (own + o) % experts
        return copy(outs.at[t, to], returned[t].at[own], ry_send.at[t, o], ry_recv.at[t, o], dp, to)

    def rc_copy(k, q, r):
        return copy(parts.at[k, at(q, r, 1 - c)], c_buf.at[k, q, r], rc_send.at[k, q, r],
                    rc_recv.at[k, q, r], other, own)

    def rx_copy(k, q, o):
        to = (x + o) % cross
        return copy(c_buf.at[k, q, to], x_buf.at[k, q, o - 1], rx_send.at[k, q, o],
                    rx_recv.at[k, q, o], at(z, to, c), own)

    def rz_copy(k, q, step):
        slot = q if step > 0 else jnp.where(q == z - 1, lines, q)
        return copy(c_buf.at[k, q, x], z_buf.at[k, slot], rz_send.at[k, q], rz_recv.at[k, slot],
                    at(z + step, x, c), own)

    def pair(k, q, r):
        rc_copy(k, q, r).wait_recv()
        return parts[k, at(q, r, c)].astype(f32) + c_buf[k, q, r].astype(f32)

    def make_parts(i):
        q = near(lines - 1 - i)
        for k in range(3):
            made = contract_first(slice_of(0 if k < 2 else 1, q), deltas[k])
            parts[k, pl.ds(q * per, per)] = made.astype(bf16).reshape(per, rows, width)
            for o in range(cross):
                sent.start(bind(lambda k, q, o: rc_copy(k, q, (x + 1 + o) % cross), k, q, o))

    def send_across(i):
        q = near(lines - 1 - i)
        for k in range(3):
            for o in range(1, cross):
                r = (x + o) % cross
                c_buf[k, q, r] = pair(k, q, r).astype(bf16)
                sent.start(bind(rx_copy, k, q, o))

    def outputs():
        def body(q, carry):
            def weights(k):
                return fulls[k, pl.ds(q * per, per)].reshape(wide, width)
            out = contract_last(deltas[2], weights(2)).astype(bf16)
            outs[0, :, :, lanes(q)] = out.reshape(experts, capacity, wide)
            grad = contract_last(deltas[0], weights(0)) + contract_last(deltas[1], weights(1))
            outs[1, :, :, lanes(q)] = grad.astype(bf16).reshape(experts, capacity, wide)
            return carry
        lax.fori_loop(0, lines, body, 0)
        for t in range(2):
            for o in range(1, experts):
                sent.start(bind(ry_copy, t, o))
        return [
            pltpu.make_async_copy(outs.at[t, own], returned[t].at[own], own_sem.at[t])
            for t in range(2)
        ]

    make_parts(0)
    for i in range(1, lines):
        make_parts(i)
        send_across(i - 1)
    send_across(lines - 1)
    local = outputs()
    for each in local:
        each.start()
    for i in range(lines):
        q = near(lines - 1 - i)
        for k in range(3):
            total = pair(k, q, x)
            for o in range(1, cross):
                rx_copy(k, q, o).wait_recv()
                total = total + x_buf[k, q, o - 1].astype(f32)
            acc[...] = total

            def add(slot, k=k):
                held = z_buf.at[k, slot]
                copy(held, held, rz_send.at[k, 0], rz_recv.at[k, slot], other, own).wait_recv()
                acc[...] += z_buf[k, slot].astype(f32)

            run(bind(add, q), (z > 0) & (q >= z))
            run(bind(add, jnp.where(q == z, lines, q)), (z < lines - 1) & (q <= z))

            def keep(k=k):
                totals[k] = acc[...]

            def pass_on(k=k, q=q):
                c_buf[k, q, x] = acc[...].astype(bf16)

            run(keep, q == z)
            run(pass_on, q != z)
            sent.start(bind(rz_copy, k, q, 1), q > z)
            sent.start(bind(rz_copy, k, q, -1), q < z)
    for t in range(2):
        for o in range(1, experts):
            held = returned[t].at[(own - o + experts) % experts]
            copy(held, held, ry_send.at[t, o], ry_recv.at[t, o], dp, (own + o) % experts).wait_recv()
    for each in local:
        each.wait()
    sent.finish()


def layer(lines, cross, experts, trio, to_slot, tokens, levels, grad_out):
    n = lines * cross * 2
    rows, width = trio[0].shape
    slots = to_slot.shape[0]
    capacity = slots // experts
    model_width = tokens.shape[1]
    dma = pltpu.SemaphoreType.DMA
    anywhere = pl.BlockSpec(memory_space=pl.ANY)
    inside = pl.BlockSpec(memory_space=pltpu.VMEM)
    bf16, f32 = jnp.bfloat16, jnp.float32
    back = jax.ShapeDtypeStruct((experts, capacity, model_width), bf16)
    pair = pltpu.VMEM((2, experts, capacity, model_width), bf16)
    by_shard = [dma((lines, cross, 3)) for _ in range(4)]
    by_part = [dma((3, lines, cross)) for _ in range(4)]
    swap = [dma((2, experts)), dma((2, experts))]
    totals, returned, arrived = pl.pallas_call(
        functools.partial(layer_kernel, lines, cross, experts),
        out_shape=[jax.ShapeDtypeStruct((3, rows, width), f32), back, back],
        in_specs=[anywhere] * 3 + [inside] * 4,
        out_specs=[inside, anywhere, anywhere],
        scratch_shapes=[
            pltpu.VMEM((3, n, rows, width), bf16),
            pair, pair, pair,
            pltpu.VMEM((3, slots, width), f32),
            pltpu.VMEM((3, slots, width), bf16),
            pltpu.VMEM((3, n, rows, width), bf16),
            pltpu.VMEM((3, lines, cross, rows, width), bf16),
            pltpu.VMEM((3, lines, max(1, cross - 1), rows, width), bf16),
            pltpu.VMEM((3, lines + 1, rows, width), bf16),
            pltpu.VMEM((rows, width), f32),
            dma((2, lines, 3)), dma((lines, 3)), *by_shard, *swap, dma((3,)),
            dma((3, lines)), dma((3, lines + 1)), *by_part, *swap,
        ],
        compiler_params=pltpu.CompilerParams(
            collective_id=0, has_side_effects=True, vmem_limit_bytes=VMEM_LIMIT
        ),
        name="expert_layer",
    )(*trio, to_slot, tokens, levels, grad_out)
    return totals, returned, arrived


def shards(lines, cross, tokens, routes, gate_levels, w_gate, w_up, w_down, grad_out):
    experts = lax.axis_size("expert")
    tok_rows = tokens.shape[0]
    model_width = tokens.shape[1]
    capacity = min(tok_rows, tok_rows * TOP * 5 // (4 * experts))
    capacity = -(-capacity // 16) * 16
    slot_count = experts * capacity
    expert_of = routes[:, 0]
    onehot = (expert_of[:, None] == jnp.arange(experts, dtype=jnp.int32)[None, :]).astype(jnp.bfloat16)
    place = jnp.arange(tok_rows, dtype=jnp.int32)
    earlier = jnp.dot(
        (place[:, None] > place[None, :]).astype(jnp.bfloat16), onehot,
        preferred_element_type=jnp.float32,
    )
    slot_rank = jnp.sum(earlier * onehot.astype(jnp.float32), axis=1).astype(jnp.int32)
    slot_index = expert_of * capacity + slot_rank
    to_slot = (slot_index[:, None] == jnp.arange(slot_count, dtype=jnp.int32)[None, :]).astype(
        jnp.bfloat16
    )
    gate_weight = gate_levels.astype(jnp.float32) / 64.0

    def unpack_rows(values):
        return jnp.dot(
            to_slot, values.reshape(slot_count, model_width), preferred_element_type=jnp.float32
        )

    totals, returned, arrived = layer(
        lines, cross, experts, (w_gate[0], w_up[0], w_down[0]),
        to_slot.T, tokens, gate_levels, grad_out,
    )
    moe_out = (gate_weight * unpack_rows(returned)).astype(jnp.bfloat16)
    grad_tokens = unpack_rows(arrived).astype(jnp.bfloat16)
    return (moe_out, grad_tokens, totals[0:1], totals[1:2], totals[2:3])


def solution(mesh):
    chips = mesh.shape["dp"] // 2
    lines = 4 if chips % 4 == 0 else chips
    in_specs = (
        P(("dp", "expert"), None),
        P(("dp", "expert"), None),
        P(("dp", "expert"), None),
        P("expert", "dp", None),
        P("expert", "dp", None),
        P("expert", "dp", None),
        P(("dp", "expert"), None),
    )
    out_specs = (
        P(("dp", "expert"), None),
        P(("dp", "expert"), None),
        P("expert", "dp", None),
        P("expert", "dp", None),
        P("expert", "dp", None),
    )
    return jax.shard_map(
        functools.partial(shards, lines, chips // lines),
        mesh=mesh, in_specs=in_specs, out_specs=out_specs, check_vma=False,
    )
```

time: 398 us -> 160 us (0.40)
  waiting for transfers between devices: 269 us -> 0 us
  Pallas kernels: 0 us -> 147 us
  matrix products: 41.8 us -> 6.41 us
  blocking collectives: 24.7 us -> 0 us
  local copies, waits for them, and re-layouts: 18.6 us -> 2.62 us
  other arithmetic: 16.2 us -> 2.07 us
  between operations: 14.3 us -> 0.66 us
  starting transfers between devices: 12.6 us -> 0 us
    pallas_call x0 -> x1, Pallas kernels: none -> 147 us  [layer(): pl.pallas_call(functools.partial(layer_kernel, lines, cross, experts), ou...]
    reduce_scatter x3 -> x0, waiting for transfers between devices: 139 us -> none  [the longest x1 71.4 us: shards(): lax.psum_scatter(part_down, 'dp', scatter_dimension=0, tiled=True)]
    all_gather x3 -> x0, waiting for transfers between devices: 95.9 us -> none  [the longest x1 45.2 us: shards(): lax.all_gather(w_down, 'dp', axis=1, tiled=True)]
    dot_general x9 -> x3, matrix products: 41.8 us -> 6.41 us  [the longest x2 5.46 us: unpack_rows(): jnp.dot(to_slot, values.reshape(slot_count, model_width), preferred_eleme...]
    all_to_all x3 -> x0, waiting for transfers between devices: 31.4 us -> none  [the longest x1 17.3 us: shards(): lax.all_to_all(token_grad.reshape(experts, capacity, model_width), 'exper...]
    all_to_all x1 -> x0, blocking collectives: 24.7 us -> none  [shards(): lax.all_to_all(pack_rows(tokens), 'expert', split_axis=0, concat_axis=0,...]
    gather x4 -> x0, local copies, waits for them, and re-layouts: 13.3 us -> none  [the longest x2 6.4 us: pack_rows(): jnp.take(values, source_row, axis=0) * filled]
    all_to_all x3 -> x0, starting transfers between devices: 12.2 us -> none  [the longest x1 4.8 us: shards(): lax.all_to_all(token_grad.reshape(experts, capacity, model_width), 'exper...]
  transfers between devices with their start and end apart: 9 -> 0, of which waited for: 7 -> 0; matrix products, arithmetic and copies ran while one was open for 16% -> 0% of each run, Pallas kernels for 0% -> 0%
where the time goes in v2:
time: 160 us; the launch traced here: 159 us
  Pallas kernels  147 us (92%)
  matrix products  6.41 us (4%)
  local copies, waits for them, and re-layouts  2.62 us (2%)
  other arithmetic  2.07 us (1%)
    pallas_call x1, Pallas kernels, layer(): pl.pallas_call(functools.partial(layer_kernel, lines, cross, experts), ou...  147 us
    dot_general x2, matrix products, unpack_rows(): jnp.dot(to_slot, values.reshape(slot_count, model_width), preferred_eleme...  5.46 us

profile of v2, /device:TPU:0, one launch (start us, length us, event | category | flops | bytes accessed | tf_op | source)
XLA Modules:
  0.0 158.8 jit_solution(5120644565476570865)
XLA Ops:
  0.6 1.0 fusion.1
  1.6 0.7 multiply_add_fusion
  2.3 0.7 convert_multiply_fusion
  3.0 1.5 copy.12.refs_5_
  4.4 0.7 fusion.2.refs_3_
  5.1 147.0 %expert_layer.1 = (f32[3,160,768]{2,1,0:T(8,128)}, bf16[2,160,2560]{2,1,0:T(8,128)(2,1)}, bf16[2,160,2560]{2,1,0:T(8,128)(2,1)}) custom-call(bf16[160,768]{1,0:T(8,128)(2,1)} %bitcast.12, bf16[160,768]{1,0:T(8,128)(2,1)} %bitcast.13, bf16[160,768]{1,0:T(8,128)(2,1)} %bitcast.14, bf16[320,256]{1,0:T(8,128)(2,1)} %fusion.2.refs_3_, bf16[256,2560]{1,0:T(8,128)(2,1)} %refs_4_.1, ...), custom_call_target="tpu_custom_call" | custom-call | tf_op jit(solution)/shard_map/expert_layer/pallas_call | solution.py:336
  152.2 0.0 copy-start
  152.2 3.5 %fusion = bf16[256,2560]{1,0:T(8,128)(2,1)} fusion(bf16[320,2560]{1,0:T(8,128)(2,1)} %bitcast.21, f32[256]{0:T(256)S(1)} %bitcast.20, s32[256]{0:T(256)S(1)} %bitcast.16), kind=kOutput, calls=%fused_computation.1 | convolution fusion | flops 420823040 | bytes 2951168 | tf_op jit(solution)/shard_map/dot_general | solution.py:384
  155.7 0.0 copy-start.1
  155.7 0.0 copy-done
  155.7 2.0 %convolution_convert_fusion = bf16[256,2560]{1,0:T(8,128)(2,1)} fusion(bf16[320,2560]{1,0:T(8,128)(2,1)S(1)} %bitcast.11, s32[256]{0:T(256)S(1)} %bitcast.17), kind=kOutput, calls=%fused_computation.2 | convolution fusion | flops 420167680 | bytes 2950144 | tf_op jit(solution)/shard_map/dot_general | solution.py:384
  157.7 0.0 copy-done.1
  157.7 1.1 fusion.7
  (1 shorter events, 0.0 us)
Async XLA Ops:
  152.2 3.5 %copy-start = (bf16[2,160,2560]{2,1,0:T(8,128)(2,1)S(1)}, bf16[2,160,2560]{2,1,0:T(8,128)(2,1)}, u32[]{:S(2)}) copy-start(bf16[2,160,2560]{2,1,0:T(8,128)(2,1)} %get-tuple-element.9) | copy-start | bytes 4915204
  155.7 2.0 %copy-start.1 = (f32[3,160,768]{2,1,0:T(8,128)S(1)}, f32[3,160,768]{2,1,0:T(8,128)}, u32[]{:S(2)}) copy-start(f32[3,160,768]{2,1,0:T(8,128)} %get-tuple-element.10) | copy-start | bytes 4423684

commit v3 on v2

--- a/solution.py
+++ b/solution.py
@@ -69,11 +69,11 @@
 
 
 def layer_kernel(lines, cross, experts, *refs):
-    shards, to_slot, tokens, levels, grad_out, totals = refs[0:3], refs[3], refs[4], refs[5], refs[6], refs[7]
-    returned = refs[8:10]
-    fulls, blocks, landed, outs, acts, deltas, parts, c_buf, x_buf, z_buf, acc = refs[10:21]
+    shards, routes, levels, tokens, grad_out = refs[0:3], refs[3], refs[4], refs[5], refs[6]
+    totals, rows_out = refs[7], refs[8:10]
+    fulls, blocks, landed, returned, to_slot, acts, deltas, parts, c_buf, x_buf, z_buf, acc = refs[10:22]
     (z_send, z_recv, x_send, x_recv, c_send, c_recv, y_send, y_recv, own_sem,
-     rz_send, rz_recv, rx_send, rx_recv, rc_send, rc_recv, ry_send, ry_recv) = refs[21:]
+     rz_send, rz_recv, rx_send, rx_recv, rc_send, rc_recv, ry_send, ry_recv) = refs[22:]
     dp, own, z, x, c = places(lines, cross)
     other = dp + 1 - 2 * c
     per = 2 * cross
@@ -127,18 +127,28 @@
     for each in local:
         each.start()
 
+    tok_rows = tokens.shape[0]
+    expert_row = routes[...]
+    some = (max(16, experts), tok_rows)
+    chosen = (lax.broadcasted_iota(jnp.int32, some, 0) == expert_row).astype(f32)
+    square = (tok_rows, tok_rows)
+    before = lax.broadcasted_iota(jnp.int32, square, 0) < lax.broadcasted_iota(jnp.int32, square, 1)
+    earlier = jnp.dot(chosen.astype(bf16), before.astype(f32).astype(bf16), preferred_element_type=f32)
+    rank = jnp.sum(earlier * chosen, axis=0, keepdims=True).astype(jnp.int32)
+    slot = expert_row * capacity + rank
+    placed = (lax.broadcasted_iota(jnp.int32, (slots, tok_rows), 0) == slot).astype(f32)
+    to_slot[0] = placed.astype(bf16)
+    to_slot[1] = (placed * (levels[...].astype(f32) / 64.0)).astype(bf16)
+
     for t in range(2):
         def pack(q, carry, t=t):
             values = (tokens, grad_out)[t][:, lanes(q)]
-            if t == 1:
-                weight = levels[...].astype(f32) / 64.0
-                values = (weight * values.astype(f32)).astype(bf16)
-            packed = jnp.dot(to_slot[...], values, preferred_element_type=f32).astype(bf16)
+            packed = jnp.dot(to_slot[t], values, preferred_element_type=f32).astype(bf16)
             blocks[t, :, :, lanes(q)] = packed.reshape(experts, capacity, wide)
             return carry
         lax.fori_loop(0, lines, pack, 0)
         for o in range(1, experts):
-            sent.start(bind(y_copy, t, o))
+            y_copy(t, o).start()
         landed[t, own] = blocks[t, own]
     for each in local:
         each.wait()
@@ -170,9 +180,9 @@
     def slice_of(t, q):
         return landed[t, :, :, lanes(q)].reshape(slots, wide)
 
-    def forward(j):
+    def forward(j, kinds):
         q = near(j)
-        for k in range(3):
+        for k in kinds:
             for r in range(cross):
                 held = fulls.at[k, at(q, r, 1 - c)]
                 copy(held, held, c_send.at[q, r, k], c_recv.at[q, r, k], other, own).wait_recv()
@@ -180,9 +190,13 @@
             more = jnp.dot(slice_of(0 if k < 2 else 1, q), weights, preferred_element_type=f32)
             acts[k] = more if j == 0 else acts[k] + more
 
-    done = 0
-    for s in range(1, lines + 1):
-        for k in range(3):
+    def y_arrived(t):
+        for o in range(1, experts):
+            held = landed.at[t, (own - o + experts) % experts]
+            copy(held, held, y_send.at[t, o], y_recv.at[t, o], dp, (own + o) % experts).wait_recv()
+
+    def gather_step(s, kinds):
+        for k in kinds:
             if s < lines:
                 from_z(k, z - s, 1, z >= s)
                 from_z(k, z + s, -1, z + s < lines)
@@ -191,36 +205,42 @@
             else:
                 from_x(k, z - (s - 1), z >= s - 1)
                 from_x(k, z + (s - 1), z + s - 1 < lines)
+
+    done = 0
+    for s in range(1, lines + 1):
+        gather_step(s, (0, 1))
         if s == max(1, lines // 2):
-            for t in range(2):
-                for o in range(1, experts):
-                    held = landed.at[t, (own - o + experts) % experts]
-                    copy(held, held, y_send.at[t, o], y_recv.at[t, o], dp, (own + o) % experts).wait_recv()
+            y_arrived(0)
         if s >= max(1, lines // 2):
             last = {lines: lines, lines - 1: lines - 1}.get(s, s - 1)
             while done < last:
-                forward(done)
+                forward(done, (0, 1))
                 done += 1
+    y_arrived(1)
 
     step_rows = 32
 
-    def middle(b, carry):
-        block = pl.ds(pl.multiple_of(b * step_rows, step_rows), step_rows)
-        act_gate, act_up, hidden_grad = acts[0, block], acts[1, block], acts[2, block]
+    def block_of(b):
+        return pl.ds(pl.multiple_of(b * step_rows, step_rows), step_rows)
+
+    def make_hidden(b, carry):
+        act_gate, act_up = acts[0, block_of(b)], acts[1, block_of(b)]
+        deltas[2, block_of(b)] = (act_gate * jax.nn.sigmoid(act_gate) * act_up).astype(bf16)
+        return carry
+
+    def make_deltas(b, carry):
+        act_gate, act_up, hidden_grad = (acts[k, block_of(b)] for k in range(3))
         sigmoid_gate = jax.nn.sigmoid(act_gate)
         silu_gate = act_gate * sigmoid_gate
-        deltas[0, block] = (
+        deltas[0, block_of(b)] = (
             hidden_grad * act_up * sigmoid_gate * (1.0 + act_gate * (1.0 - sigmoid_gate))
         ).astype(bf16)
-        deltas[1, block] = (hidden_grad * silu_gate).astype(bf16)
-        deltas[2, block] = (silu_gate * act_up).astype(bf16)
+        deltas[1, block_of(b)] = (hidden_grad * silu_gate).astype(bf16)
         return carry
-
-    lax.fori_loop(0, slots // step_rows, middle, 0)
 
     def ry_copy(t, o):
         to = (own + o) % experts
-        return copy(outs.at[t, to], returned[t].at[own], ry_send.at[t, o], ry_recv.at[t, o], dp, to)
+        return copy(blocks.at[t, to], returned.at[t, own], ry_send.at[t, o], ry_recv.at[t, o], dp, to)
 
     def rc_copy(k, q, r):
         return copy(parts.at[k, at(q, r, 1 - c)], c_buf.at[k, q, r], rc_send.at[k, q, r],
@@ -240,107 +260,130 @@
         rc_copy(k, q, r).wait_recv()
         return parts[k, at(q, r, c)].astype(f32) + c_buf[k, q, r].astype(f32)
 
-    def make_parts(i):
+    def make_parts(i, kinds):
         q = near(lines - 1 - i)
-        for k in range(3):
+        for k in kinds:
             made = contract_first(slice_of(0 if k < 2 else 1, q), deltas[k])
             parts[k, pl.ds(q * per, per)] = made.astype(bf16).reshape(per, rows, width)
             for o in range(cross):
                 sent.start(bind(lambda k, q, o: rc_copy(k, q, (x + 1 + o) % cross), k, q, o))
 
-    def send_across(i):
+    def send_across(i, kinds):
         q = near(lines - 1 - i)
-        for k in range(3):
+        for k in kinds:
             for o in range(1, cross):
                 r = (x + o) % cross
                 c_buf[k, q, r] = pair(k, q, r).astype(bf16)
                 sent.start(bind(rx_copy, k, q, o))
 
     def outputs():
+        for t in range(2):
+            for o in range(1, experts):
+                y_copy(t, o).wait_send()
+
         def body(q, carry):
             def weights(k):
                 return fulls[k, pl.ds(q * per, per)].reshape(wide, width)
             out = contract_last(deltas[2], weights(2)).astype(bf16)
-            outs[0, :, :, lanes(q)] = out.reshape(experts, capacity, wide)
+            blocks[0, :, :, lanes(q)] = out.reshape(experts, capacity, wide)
             grad = contract_last(deltas[0], weights(0)) + contract_last(deltas[1], weights(1))
-            outs[1, :, :, lanes(q)] = grad.astype(bf16).reshape(experts, capacity, wide)
+            blocks[1, :, :, lanes(q)] = grad.astype(bf16).reshape(experts, capacity, wide)
             return carry
         lax.fori_loop(0, lines, body, 0)
         for t in range(2):
             for o in range(1, experts):
                 sent.start(bind(ry_copy, t, o))
-        return [
-            pltpu.make_async_copy(outs.at[t, own], returned[t].at[own], own_sem.at[t])
-            for t in range(2)
-        ]
-
-    make_parts(0)
+            returned[t, own] = blocks[t, own]
+
+    def unpack(t):
+        for o in range(1, experts):
+            held = returned.at[t, (own - o + experts) % experts]
+            copy(held, held, ry_send.at[t, o], ry_recv.at[t, o], dp, (own + o) % experts).wait_recv()
+
+        def body(q, carry):
+            values = returned[t, :, :, lanes(q)].reshape(slots, wide)
+            rows_out[t][:, lanes(q)] = contract_first(to_slot[1 - t], values).astype(bf16)
+            return carry
+        lax.fori_loop(0, lines, body, 0)
+
+    def along(i, k):
+        q = near(lines - 1 - i)
+        total = pair(k, q, x)
+        for o in range(1, cross):
+            rx_copy(k, q, o).wait_recv()
+            total = total + x_buf[k, q, o - 1].astype(f32)
+        acc[...] = total
+
+        def add(slot):
+            held = z_buf.at[k, slot]
+            copy(held, held, rz_send.at[k, 0], rz_recv.at[k, slot], other, own).wait_recv()
+            acc[...] += z_buf[k, slot].astype(f32)
+
+        run(bind(add, q), (z > 0) & (q >= z))
+        run(bind(add, jnp.where(q == z, lines, q)), (z < lines - 1) & (q <= z))
+
+        def keep():
+            totals[k] = acc[...]
+
+        def pass_on():
+            c_buf[k, q, x] = acc[...].astype(bf16)
+
+        run(keep, q == z)
+        run(pass_on, q != z)
+        sent.start(bind(rz_copy, k, q, 1), q > z)
+        sent.start(bind(rz_copy, k, q, -1), q < z)
+
+    lax.fori_loop(0, slots // step_rows, make_hidden, 0)
+    for s in range(1, lines + 1):
+        gather_step(s, (2,))
+        make_parts(s - 1, (2,))
+        if s > 1:
+            send_across(s - 2, (2,))
+    send_across(lines - 1, (2,))
+    for j in range(lines):
+        forward(j, (2,))
+    lax.fori_loop(0, slots // step_rows, make_deltas, 0)
+    make_parts(0, (0, 1))
     for i in range(1, lines):
-        make_parts(i)
-        send_across(i - 1)
-    send_across(lines - 1)
-    local = outputs()
-    for each in local:
-        each.start()
+        make_parts(i, (0, 1))
+        send_across(i - 1, (0, 1))
+    send_across(lines - 1, (0, 1))
+    outputs()
     for i in range(lines):
-        q = near(lines - 1 - i)
-        for k in range(3):
-            total = pair(k, q, x)
-            for o in range(1, cross):
-                rx_copy(k, q, o).wait_recv()
-                total = total + x_buf[k, q, o - 1].astype(f32)
-            acc[...] = total
-
-            def add(slot, k=k):
-                held = z_buf.at[k, slot]
-                copy(held, held, rz_send.at[k, 0], rz_recv.at[k, slot], other, own).wait_recv()
-                acc[...] += z_buf[k, slot].astype(f32)
-
-            run(bind(add, q), (z > 0) & (q >= z))
-            run(bind(add, jnp.where(q == z, lines, q)), (z < lines - 1) & (q <= z))
-
-            def keep(k=k):
-                totals[k] = acc[...]
-
-            def pass_on(k=k, q=q):
-                c_buf[k, q, x] = acc[...].astype(bf16)
-
-            run(keep, q == z)
-            run(pass_on, q != z)
-            sent.start(bind(rz_copy, k, q, 1), q > z)
-            sent.start(bind(rz_copy, k, q, -1), q < z)
-    for t in range(2):
-        for o in range(1, experts):
-            held = returned[t].at[(own - o + experts) % experts]
-            copy(held, held, ry_send.at[t, o], ry_recv.at[t, o], dp, (own + o) % experts).wait_recv()
-    for each in local:
-        each.wait()
+        along(i, 2)
+    for i in range(lines):
+        for k in (0, 1):
+            along(i, k)
+        if i == max(0, lines - 3):
+            unpack(0)
+        if i == max(0, lines - 2):
+            unpack(1)
     sent.finish()
 
 
-def layer(lines, cross, experts, trio, to_slot, tokens, levels, grad_out):
+def layer(lines, cross, experts, capacity, trio, routes, levels, tokens, grad_out):
     n = lines * cross * 2
     rows, width = trio[0].shape
-    slots = to_slot.shape[0]
-    capacity = slots // experts
-    model_width = tokens.shape[1]
+    slots = experts * capacity
+    tok_rows, model_width = tokens.shape
     dma = pltpu.SemaphoreType.DMA
     anywhere = pl.BlockSpec(memory_space=pl.ANY)
     inside = pl.BlockSpec(memory_space=pltpu.VMEM)
     bf16, f32 = jnp.bfloat16, jnp.float32
-    back = jax.ShapeDtypeStruct((experts, capacity, model_width), bf16)
+    back = jax.ShapeDtypeStruct((tok_rows, model_width), bf16)
     pair = pltpu.VMEM((2, experts, capacity, model_width), bf16)
     by_shard = [dma((lines, cross, 3)) for _ in range(4)]
     by_part = [dma((3, lines, cross)) for _ in range(4)]
     swap = [dma((2, experts)), dma((2, experts))]
-    totals, returned, arrived = pl.pallas_call(
+    return pl.pallas_call(
         functools.partial(layer_kernel, lines, cross, experts),
         out_shape=[jax.ShapeDtypeStruct((3, rows, width), f32), back, back],
         in_specs=[anywhere] * 3 + [inside] * 4,
-        out_specs=[inside, anywhere, anywhere],
+        out_specs=[inside] * 3,
         scratch_shapes=[
             pltpu.VMEM((3, n, rows, width), bf16),
             pair, pair, pair,
+            pltpu.VMEM((2, slots, tok_rows), bf16),
             pltpu.VMEM((3, slots, width), f32),
             pltpu.VMEM((3, slots, width), bf16),
             pltpu.VMEM((3, n, rows, width), bf16),
@@ -355,42 +398,18 @@
             collective_id=0, has_side_effects=True, vmem_limit_bytes=VMEM_LIMIT
         ),
         name="expert_layer",
-    )(*trio, to_slot, tokens, levels, grad_out)
-    return totals, returned, arrived
+    )(*trio, routes, levels, tokens, grad_out)
 
 
 def shards(lines, cross, tokens, routes, gate_levels, w_gate, w_up, w_down, grad_out):
     experts = lax.axis_size("expert")
     tok_rows = tokens.shape[0]
-    model_width = tokens.shape[1]
     capacity = min(tok_rows, tok_rows * TOP * 5 // (4 * experts))
     capacity = -(-capacity // 16) * 16
-    slot_count = experts * capacity
-    expert_of = routes[:, 0]
-    onehot = (expert_of[:, None] == jnp.arange(experts, dtype=jnp.int32)[None, :]).astype(jnp.bfloat16)
-    place = jnp.arange(tok_rows, dtype=jnp.int32)
-    earlier = jnp.dot(
-        (place[:, None] > place[None, :]).astype(jnp.bfloat16), onehot,
-        preferred_element_type=jnp.float32,
-    )
-    slot_rank = jnp.sum(earlier * onehot.astype(jnp.float32), axis=1).astype(jnp.int32)
-    slot_index = expert_of * capacity + slot_rank
-    to_slot = (slot_index[:, None] == jnp.arange(slot_count, dtype=jnp.int32)[None, :]).astype(
-        jnp.bfloat16
-    )
-    gate_weight = gate_levels.astype(jnp.float32) / 64.0
-
-    def unpack_rows(values):
-        return jnp.dot(
-            to_slot, values.reshape(slot_count, model_width), preferred_element_type=jnp.float32
-        )
-
-    totals, returned, arrived = layer(
-        lines, cross, experts, (w_gate[0], w_up[0], w_down[0]),
-        to_slot.T, tokens, gate_levels, grad_out,
-    )
-    moe_out = (gate_weight * unpack_rows(returned)).astype(jnp.bfloat16)
-    grad_tokens = unpack_rows(arrived).astype(jnp.bfloat16)
+    totals, moe_out, grad_tokens = layer(
+        lines, cross, experts, capacity, (w_gate[0], w_up[0], w_down[0]),
+        routes.reshape(1, tok_rows), gate_levels.reshape(1, tok_rows), tokens, grad_out,
+    )
     return (moe_out, grad_tokens, totals[0:1], totals[1:2], totals[2:3])
 
 

time: 160 us -> 166 us (1.038)
  Pallas kernels: 147 us -> 160 us
  matrix products: 6.41 us -> 0 us
  local copies, waits for them, and re-layouts: 2.62 us -> 5.41 us
  other arithmetic: 2.07 us -> 0 us
    pallas_call x1, Pallas kernels: 147 us -> 160 us  [layer(): pl.pallas_call(functools.partial(layer_kernel, lines, cross, experts), ou...]
    dot_general x3 -> x0, matrix products: 6.41 us -> none  [the longest x2 5.46 us: unpack_rows(): jnp.dot(to_slot, values.reshape(slot_count, model_width), preferred_eleme...]
where the time goes in v3:
time: 166 us
  Pallas kernels  160 us (96%)
  local copies, waits for them, and re-layouts  5.41 us (3%)
    pallas_call x1, Pallas kernels, layer(): pl.pallas_call(functools.partial(layer_kernel, lines, cross, experts), ou...  160 us

profile of v3, /device:TPU:0, one launch (start us, length us, event | category | flops | bytes accessed | tf_op | source)
XLA Modules:
  0.0 166.1 jit_solution(191300002451269793)
XLA Ops:
  0.6 160.0 %expert_layer.1 = (f32[3,160,768]{2,1,0:T(8,128)}, bf16[256,2560]{1,0:T(8,128)(2,1)}, bf16[256,2560]{1,0:T(8,128)(2,1)}) custom-call(bf16[160,768]{1,0:T(8,128)(2,1)} %bitcast.5, bf16[160,768]{1,0:T(8,128)(2,1)} %bitcast.6, bf16[160,768]{1,0:T(8,128)(2,1)} %bitcast.7, s32[1,256]{1,0:T(1,128)} %bitcast.8, s32[1,256]{1,0:T(1,128)} %bitcast.9, ...), custom_call_target="tpu_custom_call" | custom-call | tf_op jit(solution)/shard_map/expert_layer/pallas_call | solution.py:378
  160.7 0.0 copy-start.1
  160.7 2.6 %fusion = (f32[1,160,768]{2,1,0:T(8,128)}, f32[1,160,768]{2,1,0:T(8,128)}, f32[1,160,768]{2,1,0:T(8,128)}) fusion(f32[3,160,768]{2,1,0:T(8,128)} %get-tuple-element.10), kind=kLoop, calls=%fused_computation | loop fusion | bytes 2949120 | tf_op jit(solution)/shard_map/slice | solution.py:413
  163.3 0.0 copy-done.1
  163.3 0.0 copy-start
  163.3 1.1 copy.14
  164.3 0.7 copy-done
  165.1 1.1 copy.15
Async XLA Ops:
  160.7 2.6 %copy-start.1 = (bf16[256,2560]{1,0:T(8,128)(2,1)S(1)}, bf16[256,2560]{1,0:T(8,128)(2,1)}, u32[]{:S(2)}) copy-start(bf16[256,2560]{1,0:T(8,128)(2,1)} %get-tuple-element.19) | copy-start | bytes 3932164
  163.3 1.8 %copy-start = (bf16[256,2560]{1,0:T(8,128)(2,1)S(1)}, bf16[256,2560]{1,0:T(8,128)(2,1)}, u32[]{:S(2)}) copy-start(bf16[256,2560]{1,0:T(8,128)(2,1)} %get-tuple-element.20) | copy-start | bytes 3932164
